TPU v7x, 32 devices: a whole 2x2x4 slice. The times are simulated.
32 devices in a mesh: groups: 2 (over x), wide: 8 (over z, y), narrow: 2 (over core).
Axes of the slice: x: 2, y: 2, z: 4, core: 2. Of those that a mesh axis runs over, the one named last changes fastest.
Arguments:
- tokens: bfloat16 [6656, 7168], P(('groups', 'wide', 'narrow')), parts along dimension 0, may hold values from -6 to 6
- norm_gain: float32 [7168], replicated, may hold values from 0.1 to 1.9
- routes: int32 [6656, 2], P(('groups', 'wide', 'narrow')), parts along dimension 0, may hold values from 0 to 127, all different within a row
- router_logits: float32 [6656, 2], P(('groups', 'wide', 'narrow')), parts along dimension 0, may hold values from -6 to 6
- gate_proj: bfloat16 [2, 7168, 4864], P('narrow', None, 'wide'), may hold values from -0.0625 to 0.0625
- up_proj: bfloat16 [2, 7168, 4864], P('narrow', None, 'wide'), may hold values from -0.0625 to 0.0625
- down_proj: bfloat16 [2, 4864, 7168], P('narrow', 'wide'), may hold values from -0.078125 to 0.078125
Outputs:
- layer_out: bfloat16 [6656, 7168], P(('groups', 'wide', 'narrow')), parts along dimension 0
There are 2 independent parts, one for each index of `groups`. A program takes and returns all parts, laid end to end along the dimension named above; an argument that names none is the same for every part. Nothing has to cross between parts.
Inputs may be any that keep to these rules, and one draw needn't show every extreme that they name: `routes`: each token names two different experts.
All inputs are finite; a program needn't handle non-finite values.
Results may differ from a plain program's by a relative error of at most 0.006.
Values may be sent and summed in bfloat16 or wider, within the bound.
A program may use at most 128 MiB of HBM per device.

v0:
```python
import jax
import jax.numpy as jnp
from jax import lax
from jax.sharding import PartitionSpec as P

CAP = 8


def normalize(tokens, norm_gain):
    wide_tok = tokens.astype(jnp.float32)
    scale = lax.rsqrt(jnp.mean(wide_tok * wide_tok, axis=1, keepdims=True) + 1e-05)
    return (wide_tok * scale * norm_gain).astype(jnp.bfloat16)


def slot_tables(routes, router_logits, flight, capacity):
    probs = jax.nn.softmax(router_logits, axis=1)
    expert_ids = lax.broadcasted_iota(jnp.int32, (1, 1, flight), 2)
    hits = routes[:, :, None] == expert_ids
    matched = jnp.sum(hits.astype(jnp.int32), axis=1)
    slot_rank = jnp.cumsum(matched, axis=0) - 1
    is_kept = (matched > 0) & (slot_rank < capacity)
    slot_ids = lax.broadcasted_iota(jnp.int32, (1, 1, capacity), 2)
    select = is_kept[:, :, None] & (slot_rank[:, :, None] == slot_ids)
    weights = jnp.sum(hits.astype(jnp.float32) * probs[:, :, None], axis=1) * is_kept.astype(
        jnp.float32
    )
    return (select, weights)


def expert_hidden(rows, gate_local, up_local):
    gate_act = jnp.dot(rows, gate_local, preferred_element_type=jnp.float32)
    up_act = jnp.dot(rows, up_local, preferred_element_type=jnp.float32)
    return (jax.nn.silu(gate_act) * up_act).astype(jnp.bfloat16)


def shards(tokens, norm_gain, routes, router_logits, gate_proj, up_proj, down_proj):
    flight = lax.axis_size("narrow")
    normed = normalize(tokens, norm_gain)
    select, weights = slot_tables(routes, router_logits, flight, CAP)
    buffer = jnp.einsum(
        "tfc,td->fcd", select.astype(jnp.bfloat16), normed, preferred_element_type=jnp.float32
    ).astype(jnp.bfloat16)
    gate_local = gate_proj[0]
    up_local = up_proj[0]
    owned = lax.all_to_all(buffer, "narrow", split_axis=0, concat_axis=1, tiled=True)
    hidden_all = expert_hidden(
        lax.all_gather(owned, "wide", axis=1, tiled=True)[0], gate_local, up_local
    )
    down_local = down_proj[0]
    summed = lax.psum_scatter(
        jnp.dot(hidden_all, down_local, preferred_element_type=jnp.float32).astype(jnp.bfloat16),
        "wide",
        scatter_dimension=0,
        tiled=True,
    )
    expert_out = summed.reshape(flight, CAP, summed.shape[1])
    returned = lax.all_to_all(expert_out, "narrow", split_axis=0, concat_axis=0, tiled=True)
    coefs = select.astype(jnp.float32) * weights[:, :, None]
    combined = jnp.einsum(
        "tfc,fcd->td", coefs, returned.astype(jnp.float32), precision=lax.Precision.HIGHEST
    )
    return (tokens.astype(jnp.float32) + combined).astype(jnp.bfloat16)


def solution(mesh):
    placed = (
        P(("groups", "wide", "narrow"), None),
        P(),
        P(("groups", "wide", "narrow"), None),
        P(("groups", "wide", "narrow"), None),
        P("narrow", None, "wide"),
        P("narrow", None, "wide"),
        P("narrow", "wide", None),
    )
    return jax.shard_map(
        shards,
        mesh=mesh,
        in_specs=placed,
        out_specs=P(("groups", "wide", "narrow"), None),
        check_vma=False,
    )
```

profile of v0, /device:TPU:0, one launch (start us, length us, event | category | flops | bytes accessed | tf_op | source)
XLA Modules:
  0.0 173.9 jit_solution(3884899779957543420)
XLA Ops:
  6.5 0.0 all-gather.2.cloned.1.call-start
  6.5 0.7 reduce_max.9
  7.2 0.7 fusion.50
  7.9 0.7 fusion.49
  8.6 0.7 convert_reduce_fusion
  9.3 0.7 select_reduce_fusion
  10.0 2.5 %fusion.10 = f32[208]{0:T(256)S(1)} fusion(bf16[208,7168]{1,0:T(8,128)(2,1)} %param.7), kind=kLoop, calls=%fused_computation.13 | loop fusion | flops 4472624 | bytes 2982720 | tf_op jit(solution)/shard_map/reduce_sum | solution.py:11
  12.6 0.6 reduce-window.6
  13.2 0.2 slice_reduce_fusion
  13.4 0.2 reduce-window.9
  13.6 0.1 add_bitcast_fusion
  13.7 2.7 %convolution_convert_fusion = bf16[2,8,7168]{2,1,0:T(8,128)(2,1)S(1)} fusion(bf16[208,7168]{1,0:T(8,128)(2,1)} %param.7, f32[7168]{0:T(1024)} %param.8, f32[208]{0:T(256)S(1)} %add_rsqrt_fusion, s32[208,2]{0,1:T(2,128)S(1)} %slice_add_fusion, pred[208,2]{0,1:T(4,128)(4,1)S(1)} %get-tuple-element.6), kind=kOutput, calls=%fused_computation.12 | convolution fusion | flops 53795328 | bytes 3242848 | tf_op jit(solution)/shard_map/tfc,td->fcd/dot_general | solution.py:40
  16.4 4.6 %all_to_all.17 = bf16[2,8,7168]{2,1,0:T(8,128)(2,1)} all-to-all(bf16[2,8,7168]{2,1,0:T(8,128)(2,1)S(1)} %convolution_convert_fusion), channel_id=1, replica_groups=mesh['groups'=2,'wide'=8,'narrow'=2] {'narrow'}, dimensions={0} | all-to-all | bytes 458752 | tf_op jit(solution)/shard_map/all_to_all | solution.py:45
  21.0 0.0 all-gather.2.cloned.1.call-update
  21.1 0.0 reduce-scatter.2.cloned.1.call-start
  21.1 49.0 %all-gather.2.cloned.1.call-done = bf16[1,128,7168]{2,1,0:T(8,128)(2,1)} async-done(((bf16[1,16,7168]{2,1,0:T(8,128)(2,1)}), bf16[1,128,7168]{2,1,0:T(8,128)(2,1)}) %all-gather.2.cloned.1.call-update) | async-done | bytes 1835024 | tf_op jit(solution)/shard_map/all_gather | solution.py:47
  70.2 0.0 copy-start
  70.2 6.6 %fusion.5 = f32[128,608]{0,1:T(8,128)S(1)} fusion(bf16[1,7168,608]{1,2,0:T(8,128)(2,1)} %param.11, bf16[1,128,7168]{2,1,0:T(8,128)(2,1)} %all-gather.2.cloned.1.call-done), kind=kOutput, calls=%fused_computation.9 | convolution fusion | flops 1115684864 | bytes 10862592 | tf_op jit(solution)/shard_map/dot_general | solution.py:31
  76.7 0.0 copy-done
  76.7 13.9 %fusion.7 = bf16[128,7168]{1,0:T(8,128)(2,1)} fusion(bf16[1,608,7168]{2,1,0:T(8,128)(2,1)} %param.13, bf16[1,7168,608]{1,2,0:T(8,128)(2,1)} %param.12, bf16[1,128,7168]{2,1,0:T(8,128)(2,1)S(1)} %copy-done, f32[128,608]{0,1:T(8,128)S(1)} %fusion.5), kind=kOutput, calls=%fused_computation.11 | convolution fusion | flops 2232754176 | bytes 21413888 | tf_op jit(solution)/shard_map/dot_general | solution.py:51
  90.7 0.0 reduce-scatter.2.cloned.1.call-update
  90.7 65.3 %reduce-scatter.2.cloned.1.call-done = bf16[16,7168]{1,0:T(8,128)(2,1)} async-done(((bf16[128,7168]{1,0:T(8,128)(2,1)}), bf16[16,7168]{1,0:T(8,128)(2,1)}) %reduce-scatter.2.cloned.1.call-update) | async-done | bytes 229392 | tf_op jit(solution)/shard_map/reduce_scatter | solution.py:50
  156.0 5.0 %all_to_all.18 = bf16[2,8,7168]{2,1,0:T(8,128)(2,1)S(1)} all-to-all(bf16[2,8,7168]{2,1,0:T(8,128)(2,1)} %bitcast.51), channel_id=1, replica_groups=mesh['groups'=2,'wide'=8,'narrow'=2] {'narrow'}, dimensions={0} | all-to-all | bytes 458752 | tf_op jit(solution)/shard_map/all_to_all | solution.py:57
  161.0 6.1 %fusion = bf16[208,7168]{1,0:T(8,128)(2,1)} fusion(bf16[2,8,7168]{2,1,0:T(8,128)(2,1)S(1)} %all_to_all.18, bf16[208,7168]{1,0:T(8,128)(2,1)} %param.7, f32[208,2]{0,1:T(2,128)S(1)} %get-tuple-element.5, s32[208,2]{0,1:T(2,128)S(1)} %slice_add_fusion, pred[208,2]{0,1:T(4,128)(4,1)S(1)} %get-tuple-element.6), kind=kOutput, calls=%fused_computation.4 | convolution fusion | flops 290744064 | bytes 6196896 | tf_op jit(solution)/shard_map/tfc,fcd->td/dot_general | solution.py:59
  (6 shorter events, 0.0 us)
Async XLA Ops:
  6.5 63.6 %all-gather.2.cloned.1.call-start = ((), (), s32[]{:S(2)}) async-start(), calls=%async_computation.3 | async-start | bytes 2064384 | tf_op jit(solution)/shard_map/all_gather | solution.py:47
  21.1 134.9 %reduce-scatter.2.cloned.1.call-start = ((), (), s32[]{:S(2)}) async-start(), calls=%async_computation.4 | async-start | bytes 2064384 | tf_op jit(solution)/shard_map/reduce_scatter | solution.py:50
  70.2 6.6 %copy-start = (bf16[1,128,7168]{2,1,0:T(8,128)(2,1)S(1)}, bf16[1,128,7168]{2,1,0:T(8,128)(2,1)}, u32[]{:S(2)}) copy-start(bf16[1,128,7168]{2,1,0:T(8,128)(2,1)} %all-gather.2.cloned.1.call-done) | copy-start | bytes 5505028
Sparse Core Ops, SparseCore 0:
  21.2 48.9 all-gather.1
  90.8 65.1 reduce-scatter.1
where the time goes:
time: 174 us
  waiting for transfers between devices  114 us (66%)
  matrix products  29.3 us (17%)
  between operations  13.4 us (8%)
  blocking collectives  9.57 us (6%)
  other arithmetic  6.91 us (4%)
    reduce_scatter x1, waiting for transfers between devices, shards(): lax.psum_scatter(jnp.dot(hidden_all, down_local, preferred_element_type=j...  65.3 us
    all_gather x1, waiting for transfers between devices, shards(): lax.all_gather(owned, 'wide', axis=1, tiled=True)[0]  49 us
    dot_general x1, matrix products, shards(): jnp.dot(hidden_all, down_local, preferred_element_type=jnp.float32)  13.9 us
    dot_general x1, matrix products, expert_hidden(): gate_act = jnp.dot(rows, gate_local, preferred_element_type=jnp.float32)  6.57 us
    dot_general x1, matrix products, shards(): jnp.einsum('tfc,fcd->td', coefs, returned.astype(jnp.float32), precision=...  6.12 us
    all_to_all x1, blocking collectives, shards(): lax.all_to_all(expert_out, 'narrow', split_axis=0, concat_axis=0, tiled=T...  4.95 us
    all_to_all x1, blocking collectives, shards(): lax.all_to_all(buffer, 'narrow', split_axis=0, concat_axis=1, tiled=True)  4.62 us
  transfers between devices with their start and end apart: 2, of which 2 were waited for; matrix products, arithmetic and copies ran while one was open for 0% of the time, Pallas kernels for 0%

commit v1 on v0

--- a/solution.py
+++ b/solution.py
@@ -1,9 +1,17 @@
+import functools
+
 import jax
 import jax.numpy as jnp
 from jax import lax
+from jax.experimental import pallas as pl
+from jax.experimental.pallas import tpu as pltpu
 from jax.sharding import PartitionSpec as P
 
 CAP = 8
+N_CHUNKS = 4
+MESH = pl.DeviceIdType.MESH
+F32 = jnp.float32
+BF16 = jnp.bfloat16
 
 
 def normalize(tokens, norm_gain):
@@ -62,6 +70,321 @@
     return (tokens.astype(jnp.float32) + combined).astype(jnp.bfloat16)
 
 
+def picks(routes, narrow):
+    count = routes.shape[1]
+    row = lax.broadcasted_iota(jnp.int32, (2 * CAP, count), 0)
+    own = row < CAP
+    expert = jnp.where(own, narrow, 1 - narrow)
+    slot = jnp.where(own, row, row - CAP)
+    first = routes[0:1, :] == expert
+    second = routes[1:2, :] == expert
+    hit = first | second
+    earlier = lax.broadcasted_iota(jnp.int32, (count, count), 0) < lax.broadcasted_iota(
+        jnp.int32, (count, count), 1
+    )
+    rank = jnp.dot(
+        jnp.where(hit, 1.0, 0.0).astype(BF16),
+        jnp.where(earlier, 1.0, 0.0).astype(BF16),
+        preferred_element_type=F32,
+    )
+    return first, second, hit & (rank == slot.astype(F32))
+
+
+def fold(rows):
+    half = rows.shape[1] // 2
+    return jnp.concatenate([rows[:, :half], rows[:, half:]], axis=0).astype(BF16)
+
+
+def unfold(packed):
+    wide = packed.astype(F32)
+    return jnp.concatenate([wide[:CAP], wide[CAP:]], axis=1)
+
+
+def experts(
+    n_z, n_c, tokens_hbm, gain, routes, gate_hbm, up_hbm, down_hbm, out,
+    tok, gate, up, down, raw, give, got, gathered, gate_acc, up_acc, hidden,
+    own_part, y_send, y_recv, z_send, z_recv, back_send, back_recv,
+    tok_sem, w_sem, d_sem, x_sem, gz_send, gz_recv, gy_send, gy_recv,
+    ry_sem, rz_send, rz_recv, b_sem,
+):
+    wide, narrow = lax.axis_index("wide"), lax.axis_index("narrow")
+    z, y = lax.div(wide, 2), lax.rem(wide, 2)
+    width = tok.shape[2]
+    rows = 2 * CAP
+    y_peer = {"wide": 2 * z + 1 - y}
+    sibling = {"narrow": 1 - narrow}
+    z_at = [lax.rem(z + step, n_z) for step in range(n_z)]
+    z_from = [lax.rem(z + n_z - step, n_z) for step in range(n_z)]
+
+    def z_peer(step):
+        return {"wide": 2 * z_at[step] + y}
+
+    def remote(source, target, send, recv, device):
+        return pltpu.make_async_remote_copy(
+            src_ref=source, dst_ref=target, send_sem=send, recv_sem=recv,
+            device_id=device, device_id_type=MESH,
+        )
+
+    def columns(k):
+        return pl.ds(pl.multiple_of(k * width, 128), width)
+
+    def token_copy(k):
+        return pltpu.make_async_copy(tokens_hbm.at[:, columns(k)], tok.at[k], tok_sem.at[k])
+
+    def weight_copies(k):
+        return (
+            pltpu.make_async_copy(gate_hbm.at[0, :, columns(k)], gate.at[k], w_sem.at[0, k]),
+            pltpu.make_async_copy(up_hbm.at[0, :, columns(k)], up.at[k], w_sem.at[1, k]),
+        )
+
+    def down_copy(k):
+        return pltpu.make_async_copy(down_hbm.at[0, :, columns(k)], down.at[k], d_sem.at[k])
+
+    def exchange(k):
+        return remote(give.at[k], got.at[k], x_sem.at[0, k], x_sem.at[1, k], sibling)
+
+    def along_z(k, step):
+        return remote(
+            gathered.at[k, z], gathered.at[k, z], gz_send.at[step, k], gz_recv.at[z, k], z_peer(step)
+        )
+
+    def from_z(k, step):
+        at = z_from[step]
+        return remote(
+            gathered.at[k, at], gathered.at[k, at], gz_send.at[step, k], gz_recv.at[at, k], z_peer(step)
+        )
+
+    def along_y(k, at):
+        return remote(
+            gathered.at[k, at], gathered.at[k, n_z + at], gy_send.at[at, k], gy_recv.at[at, k], y_peer
+        )
+
+    def sum_y(k):
+        return remote(y_send.at[k], y_recv.at[k], ry_sem.at[0, k], ry_sem.at[1, k], y_peer)
+
+    def sum_z(k, step):
+        return remote(
+            z_send.at[k, z_at[step]], z_recv.at[k, step], rz_send.at[step, k], rz_recv.at[step, k],
+            z_peer(step),
+        )
+
+    def hand_back(k):
+        return remote(back_send.at[k], back_recv.at[k], b_sem.at[0, k], b_sem.at[1, k], sibling)
+
+    for k in range(n_c):
+        token_copy(k).start()
+    barrier = pltpu.get_barrier_semaphore()
+    for peer in [sibling, y_peer] + [z_peer(step) for step in range(1, n_z)]:
+        pl.semaphore_signal(barrier, inc=1, device_id=peer, device_id_type=MESH)
+    pl.semaphore_wait(barrier, n_z + 1)
+
+    _, _, chosen = picks(routes[...], narrow)
+    chosen = jnp.where(chosen, 1.0, 0.0).astype(BF16)
+    squares = jnp.zeros((rows, 1), F32)
+    for k in range(n_c):
+        token_copy(k).wait()
+        picked = jnp.dot(chosen, tok[k], preferred_element_type=F32)
+        raw[k] = picked
+        squares = squares + jnp.sum(picked * picked, axis=1, keepdims=True)
+    for k in range(n_c):
+        for copy in weight_copies(k):
+            copy.start()
+    for k in range(n_c):
+        down_copy(k).start()
+    scale = lax.rsqrt(squares / (n_c * width) + 1e-05)
+    for k in range(n_c):
+        normed = raw[k] * scale * gain[0:1, k * width : (k + 1) * width]
+        raw[k] = normed
+        give[k] = fold(normed[CAP:])
+        exchange(k).start()
+    for k in range(n_c):
+        exchange(k).wait_recv()
+        gathered[k, z] = jnp.concatenate([raw[k, :CAP], unfold(got[k])], axis=0).astype(BF16)
+        along_y(k, z).start()
+        for step in range(1, n_z):
+            along_z(k, step).start()
+    gate_acc[...] = jnp.zeros_like(gate_acc)
+    up_acc[...] = jnp.zeros_like(up_acc)
+
+    def pass_on(k):
+        for step in range(1, n_z):
+            from_z(k, step).wait_recv()
+            along_y(k, z_from[step]).start()
+
+    pass_on(0)
+
+    def take(k, carry):
+        @pl.when(k + 1 < n_c)
+        def _():
+            pass_on(k + 1)
+
+        for step in range(n_z):
+            along_y(k, z_from[step]).wait_recv()
+        for copy in weight_copies(k):
+            copy.wait()
+        block = gathered[k].reshape(2 * n_z * rows, width)
+        gate_acc[...] += lax.dot_general(
+            block, gate[k], (((1,), (1,)), ((), ())), preferred_element_type=F32
+        )
+        up_acc[...] += lax.dot_general(
+            block, up[k], (((1,), (1,)), ((), ())), preferred_element_type=F32
+        )
+        return carry
+
+    lax.fori_loop(0, n_c, take, 0)
+    gated = gate_acc[...]
+    hidden[...] = (gated / (1.0 + jnp.exp(-gated)) * up_acc[...]).astype(BF16)
+
+    def part(k, carry):
+        down_copy(k).wait()
+        product = jnp.dot(hidden[...], down[k], preferred_element_type=F32)
+        half = n_z * rows
+        y_send[k] = product[half:].astype(BF16).reshape(n_z, rows, width)
+        sum_y(k).start()
+        own_part[k] = product[:half].reshape(n_z, rows, width)
+        return carry
+
+    lax.fori_loop(0, n_c, part, 0)
+
+    def pair_up(k):
+        sum_y(k).wait_recv()
+        both = own_part[k] + y_recv[k].astype(F32)
+        own_part[k] = both
+        z_send[k] = both.astype(BF16)
+        for step in range(1, n_z):
+            sum_z(k, step).start()
+
+    def finish(k):
+        total = own_part[k, z]
+        for step in range(1, n_z):
+            sum_z(k, step).wait_recv()
+            total = total + z_recv[k, step].astype(F32)
+        raw[k] = total
+        back_send[k] = fold(total[CAP:])
+        hand_back(k).start()
+
+    def collect(k):
+        hand_back(k).wait_recv()
+        out[:, k * width : (k + 1) * width] = jnp.concatenate(
+            [raw[k, :CAP], unfold(back_recv[k])], axis=0
+        ).astype(BF16)
+
+    pair_up(0)
+    for k in range(n_c):
+        if k + 1 < n_c:
+            pair_up(k + 1)
+        finish(k)
+        if k >= 1:
+            collect(k - 1)
+    collect(n_c - 1)
+
+    for k in range(n_c):
+        exchange(k).wait_send()
+        for step in range(n_z):
+            along_y(k, z_from[step]).wait_send()
+        for step in range(1, n_z):
+            along_z(k, step).wait_send()
+            sum_z(k, step).wait_send()
+        sum_y(k).wait_send()
+        hand_back(k).wait_send()
+
+
+def combine(narrow, routes, logits, tokens, expert_out, out, coefs):
+    @pl.when(pl.program_id(0) == 0)
+    def _():
+        first, second, chosen = picks(routes[...], narrow[0])
+        values = logits[...]
+        powers = jnp.exp(values - jnp.max(values, axis=0, keepdims=True))
+        probs = powers / jnp.sum(powers, axis=0, keepdims=True)
+        weight = jnp.where(first, probs[0:1, :], 0.0) + jnp.where(second, probs[1:2, :], 0.0)
+        rest = jnp.where(chosen, weight, 0.0)
+        for piece in range(3):
+            rounded = rest.astype(BF16)
+            coefs[piece * 2 * CAP : (piece + 1) * 2 * CAP, :] = rounded
+            rest = rest - rounded.astype(F32)
+
+    rows = expert_out[...]
+    added = lax.dot_general(
+        coefs[...],
+        jnp.concatenate([rows, rows, rows], axis=0),
+        (((0,), (0,)), ((), ())),
+        preferred_element_type=F32,
+    )
+    out[...] = (tokens[...].astype(F32) + added).astype(BF16)
+
+
+def fused(n_z, tokens, norm_gain, routes, router_logits, gate_proj, up_proj, down_proj):
+    n_c = N_CHUNKS
+    count, depth = tokens.shape
+    width = depth // n_c
+    units = gate_proj.shape[2]
+    rows = 2 * CAP
+    everyone = 2 * n_z * rows
+    vmem, hbm = pl.BlockSpec(memory_space=pltpu.VMEM), pl.BlockSpec(memory_space=pl.ANY)
+    dma = pltpu.SemaphoreType.DMA
+    routes_t, logits_t = routes.T, router_logits.T
+    expert_out = pl.pallas_call(
+        functools.partial(experts, n_z, n_c),
+        out_shape=jax.ShapeDtypeStruct((rows, depth), BF16),
+        in_specs=[hbm, vmem, vmem, hbm, hbm, hbm],
+        out_specs=vmem,
+        scratch_shapes=[
+            pltpu.VMEM((n_c, count, width), BF16),
+            pltpu.VMEM((n_c, units, width), BF16),
+            pltpu.VMEM((n_c, units, width), BF16),
+            pltpu.VMEM((n_c, units, width), BF16),
+            pltpu.VMEM((n_c, rows, width), F32),
+            pltpu.VMEM((n_c, rows, width // 2), BF16),
+            pltpu.VMEM((n_c, rows, width // 2), BF16),
+            pltpu.VMEM((n_c, 2 * n_z, rows, width), BF16),
+            pltpu.VMEM((everyone, units), F32),
+            pltpu.VMEM((everyone, units), F32),
+            pltpu.VMEM((everyone, units), BF16),
+            pltpu.VMEM((n_c, n_z, rows, width), F32),
+            pltpu.VMEM((n_c, n_z, rows, width), BF16),
+            pltpu.VMEM((n_c, n_z, rows, width), BF16),
+            pltpu.VMEM((n_c, n_z, rows, width), BF16),
+            pltpu.VMEM((n_c, n_z, rows, width), BF16),
+            pltpu.VMEM((n_c, rows, width // 2), BF16),
+            pltpu.VMEM((n_c, rows, width // 2), BF16),
+            dma((n_c,)),
+            dma((2, n_c)),
+            dma((n_c,)),
+            dma((2, n_c)),
+            dma((n_z, n_c)),
+            dma((n_z, n_c)),
+            dma((n_z, n_c)),
+            dma((n_z, n_c)),
+            dma((2, n_c)),
+            dma((n_z, n_c)),
+            dma((n_z, n_c)),
+            dma((2, n_c)),
+        ],
+        compiler_params=pltpu.CompilerParams(
+            collective_id=0, has_side_effects=True, vmem_limit_bytes=58 * 1024 * 1024
+        ),
+    )(
+        tokens, norm_gain.reshape(1, depth), routes_t,
+        jnp.swapaxes(gate_proj, 1, 2), jnp.swapaxes(up_proj, 1, 2), down_proj,
+    )
+    tile = depth // 7
+    narrow = lax.axis_index("narrow").astype(jnp.int32).reshape(1)
+    return pl.pallas_call(
+        combine,
+        grid=(7,),
+        out_shape=jax.ShapeDtypeStruct(tokens.shape, BF16),
+        in_specs=[
+            pl.BlockSpec(memory_space=pltpu.SMEM),
+            vmem,
+            vmem,
+            pl.BlockSpec((count, tile), lambda i: (0, i)),
+            pl.BlockSpec((rows, tile), lambda i: (0, i)),
+        ],
+        out_specs=pl.BlockSpec((count, tile), lambda i: (0, i)),
+        scratch_shapes=[pltpu.VMEM((3 * rows, count), BF16)],
+    )(narrow, routes_t, logits_t, tokens, expert_out)
+
+
 def solution(mesh):
     placed = (
         P(("groups", "wide", "narrow"), None),
@@ -72,8 +395,9 @@
         P("narrow", None, "wide"),
         P("narrow", "wide", None),
     )
+    fits = mesh.shape["wide"] == 8 and mesh.shape["narrow"] == 2
     return jax.shard_map(
-        shards,
+        functools.partial(fused, mesh.shape["wide"] // 2) if fits else shards,
         mesh=mesh,
         in_specs=placed,
         out_specs=P(("groups", "wide", "narrow"), None),

time: 174 us -> 73 us (0.42)
  waiting for transfers between devices: 114 us -> 0 us
  Pallas kernels: 0 us -> 72.7 us
  matrix products: 29.3 us -> 0 us
  between operations: 13.4 us -> 0.01 us
  blocking collectives: 9.57 us -> 0 us
  other arithmetic: 6.91 us -> 0 us
    pallas_call x0 -> x2, Pallas kernels: none -> 72.7 us  [the longest x1 66 us: fused(): pl.pallas_call(functools.partial(experts, n_z, n_c), out_shape=jax.ShapeD...]
    reduce_scatter x1 -> x0, waiting for transfers between devices: 65.3 us -> none  [shards(): lax.psum_scatter(jnp.dot(hidden_all, down_local, preferred_element_type=j...]
    all_gather x1 -> x0, waiting for transfers between devices: 49 us -> none  [shards(): lax.all_gather(owned, 'wide', axis=1, tiled=True)[0]]
    dot_general x4 -> x0, matrix products: 29.3 us -> none  [the longest x1 13.9 us: shards(): jnp.dot(hidden_all, down_local, preferred_element_type=jnp.float32)]
    all_to_all x2 -> x0, blocking collectives: 9.57 us -> none  [the longest x1 4.95 us: shards(): lax.all_to_all(expert_out, 'narrow', split_axis=0, concat_axis=0, tiled=T...]
    reduce_sum x4 -> x0, other arithmetic: 4.62 us -> none  [the longest x1 2.52 us: normalize(): jnp.mean(wide_tok * wide_tok, axis=1, keepdims=True) + 1e-05]
  transfers between devices with their start and end apart: 2 -> 0, of which waited for: 2 -> 0; matrix products, arithmetic and copies ran while one was open for 0% -> 0% of each run, Pallas kernels for 0% -> 0%
where the time goes in v1:
time: 73 us; the launch traced here: 72.7 us
  Pallas kernels  72.7 us (100%)
    pallas_call x1, Pallas kernels, fused(): pl.pallas_call(functools.partial(experts, n_z, n_c), out_shape=jax.ShapeD...  66 us
    pallas_call x1, Pallas kernels, fused(): pl.pallas_call(combine, grid=(7,), out_shape=jax.ShapeDtypeStruct(tokens....  6.73 us

profile of v1, /device:TPU:0, one launch (start us, length us, event | category | flops | bytes accessed | tf_op | source)
XLA Modules:
  0.0 72.7 jit_solution(6887938949685539606)
XLA Ops:
  0.0 66.0 %shard_map.73.expert_out = bf16[16,7168]{1,0:T(8,128)(2,1)} custom-call(bf16[208,7168]{1,0:T(8,128)(2,1)} %tokens.1, f32[1,7168]{1,0:T(1,128)} %bitcast.8, s32[2,208]{1,0:T(2,128)} %bitcast.9, bf16[1,608,7168]{2,1,0:T(8,128)(2,1)} %bitcast.6, bf16[1,608,7168]{2,1,0:T(8,128)(2,1)} %bitcast.7, bf16[1,608,7168]{2,1,0:T(8,128)(2,1)} %down_hbm.1), custom_call_target="tpu_custom_call" | custom-call | tf_op jit(solution)/shard_map/pallas_call | solution.py:326
  66.0 6.7 %shard_map.74 = bf16[208,7168]{1,0:T(8,128)(2,1)} custom-call(s32[1]{0:T(128)} %bitcast.narrow, s32[2,208]{1,0:T(2,128)} %bitcast.10, f32[2,208]{1,0:T(2,128)} %bitcast.11, bf16[208,7168]{1,0:T(8,128)(2,1)} %tokens.1, bf16[16,7168]{1,0:T(8,128)(2,1)} %shard_map.73.expert_out), custom_call_target="tpu_custom_call" | custom-call | tf_op jit(solution)/shard_map/pallas_call | solution.py:372

commit v2 on v1

--- a/solution.py
+++ b/solution.py
@@ -9,6 +9,7 @@
 
 CAP = 8
 N_CHUNKS = 4
+SUM_WIDTHS = (1792, 1792, 1792, 1792)
 MESH = pl.DeviceIdType.MESH
 F32 = jnp.float32
 BF16 = jnp.bfloat16
@@ -101,7 +102,7 @@
 
 
 def experts(
-    n_z, n_c, tokens_hbm, gain, routes, gate_hbm, up_hbm, down_hbm, out,
+    n_z, n_c, n_s, tokens_hbm, gain, routes, logits, gate_hbm, up_hbm, down_hbm, out, coefs,
     tok, gate, up, down, raw, give, got, gathered, gate_acc, up_acc, hidden,
     own_part, y_send, y_recv, z_send, z_recv, back_send, back_recv,
     tok_sem, w_sem, d_sem, x_sem, gz_send, gz_recv, gy_send, gy_recv,
@@ -137,8 +138,11 @@
             pltpu.make_async_copy(up_hbm.at[0, :, columns(k)], up.at[k], w_sem.at[1, k]),
         )
 
-    def down_copy(k):
-        return pltpu.make_async_copy(down_hbm.at[0, :, columns(k)], down.at[k], d_sem.at[k])
+    starts = [sum(SUM_WIDTHS[:j]) for j in range(n_s)]
+    spans = [pl.ds(starts[j], SUM_WIDTHS[j]) for j in range(n_s)]
+
+    def down_copy(j):
+        return pltpu.make_async_copy(down_hbm.at[0, :, spans[j]], down.at[:, spans[j]], d_sem.at[j])
 
     def exchange(k):
         return remote(give.at[k], got.at[k], x_sem.at[0, k], x_sem.at[1, k], sibling)
@@ -159,50 +163,69 @@
             gathered.at[k, at], gathered.at[k, n_z + at], gy_send.at[at, k], gy_recv.at[at, k], y_peer
         )
 
-    def sum_y(k):
-        return remote(y_send.at[k], y_recv.at[k], ry_sem.at[0, k], ry_sem.at[1, k], y_peer)
-
-    def sum_z(k, step):
-        return remote(
-            z_send.at[k, z_at[step]], z_recv.at[k, step], rz_send.at[step, k], rz_recv.at[step, k],
-            z_peer(step),
-        )
-
-    def hand_back(k):
-        return remote(back_send.at[k], back_recv.at[k], b_sem.at[0, k], b_sem.at[1, k], sibling)
+    def sum_y(j):
+        return remote(
+            y_send[j], y_recv[j], ry_sem.at[0, j], ry_sem.at[1, j],
+            y_peer,
+        )
+
+    def sum_z(j, step):
+        return remote(
+            z_send[j].at[z_at[step]], z_recv[j].at[step], rz_send.at[step, j],
+            rz_recv.at[step, j], z_peer(step),
+        )
+
+    def hand_back(j):
+        return remote(
+            back_send[j], back_recv[j], b_sem.at[0, j], b_sem.at[1, j],
+            sibling,
+        )
 
     for k in range(n_c):
         token_copy(k).start()
     barrier = pltpu.get_barrier_semaphore()
     for peer in [sibling, y_peer] + [z_peer(step) for step in range(1, n_z)]:
         pl.semaphore_signal(barrier, inc=1, device_id=peer, device_id_type=MESH)
-    pl.semaphore_wait(barrier, n_z + 1)
-
-    _, _, chosen = picks(routes[...], narrow)
-    chosen = jnp.where(chosen, 1.0, 0.0).astype(BF16)
+
+    first, second, kept = picks(routes[...], narrow)
+    chosen = jnp.where(kept, 1.0, 0.0).astype(BF16)
     squares = jnp.zeros((rows, 1), F32)
     for k in range(n_c):
         token_copy(k).wait()
         picked = jnp.dot(chosen, tok[k], preferred_element_type=F32)
-        raw[k] = picked
+        raw[:, k * width : (k + 1) * width] = picked
         squares = squares + jnp.sum(picked * picked, axis=1, keepdims=True)
     for k in range(n_c):
         for copy in weight_copies(k):
             copy.start()
-    for k in range(n_c):
-        down_copy(k).start()
+    for j in range(n_s):
+        down_copy(j).start()
+    pl.semaphore_wait(barrier, n_z + 1)
     scale = lax.rsqrt(squares / (n_c * width) + 1e-05)
     for k in range(n_c):
-        normed = raw[k] * scale * gain[0:1, k * width : (k + 1) * width]
-        raw[k] = normed
+        normed = raw[:, k * width : (k + 1) * width] * scale * gain[0:1, k * width : (k + 1) * width]
+        raw[:, k * width : (k + 1) * width] = normed
         give[k] = fold(normed[CAP:])
         exchange(k).start()
     for k in range(n_c):
         exchange(k).wait_recv()
-        gathered[k, z] = jnp.concatenate([raw[k, :CAP], unfold(got[k])], axis=0).astype(BF16)
+        gathered[k, z] = jnp.concatenate(
+            [raw[:CAP, k * width : (k + 1) * width], unfold(got[k])], axis=0
+        ).astype(BF16)
         along_y(k, z).start()
         for step in range(1, n_z):
             along_z(k, step).start()
+    values = logits[...]
+    powers = jnp.exp(values - jnp.max(values, axis=0, keepdims=True))
+    probs = powers / jnp.sum(powers, axis=0, keepdims=True)
+    weight = jnp.where(first, probs[0:1, :], 0.0) + jnp.where(second, probs[1:2, :], 0.0)
+    rest = jnp.where(kept, weight, 0.0)
+    pieces = []
+    for _ in range(3):
+        rounded = rest.astype(BF16).astype(F32)
+        pieces.append(rounded)
+        rest = rest - rounded
+    coefs[...] = jnp.concatenate(pieces, axis=0).T.astype(BF16)
     gate_acc[...] = jnp.zeros_like(gate_acc)
     up_acc[...] = jnp.zeros_like(up_acc)
 
@@ -235,48 +258,45 @@
     gated = gate_acc[...]
     hidden[...] = (gated / (1.0 + jnp.exp(-gated)) * up_acc[...]).astype(BF16)
 
-    def part(k, carry):
-        down_copy(k).wait()
-        product = jnp.dot(hidden[...], down[k], preferred_element_type=F32)
-        half = n_z * rows
-        y_send[k] = product[half:].astype(BF16).reshape(n_z, rows, width)
-        sum_y(k).start()
-        own_part[k] = product[:half].reshape(n_z, rows, width)
-        return carry
-
-    lax.fori_loop(0, n_c, part, 0)
-
-    def pair_up(k):
-        sum_y(k).wait_recv()
-        both = own_part[k] + y_recv[k].astype(F32)
-        own_part[k] = both
-        z_send[k] = both.astype(BF16)
-        for step in range(1, n_z):
-            sum_z(k, step).start()
-
-    def finish(k):
-        total = own_part[k, z]
-        for step in range(1, n_z):
-            sum_z(k, step).wait_recv()
-            total = total + z_recv[k, step].astype(F32)
-        raw[k] = total
-        back_send[k] = fold(total[CAP:])
-        hand_back(k).start()
-
-    def collect(k):
-        hand_back(k).wait_recv()
-        out[:, k * width : (k + 1) * width] = jnp.concatenate(
-            [raw[k, :CAP], unfold(back_recv[k])], axis=0
+    half = n_z * rows
+    for j in range(n_s):
+        down_copy(j).wait()
+        product = jnp.dot(hidden[...], down[:, spans[j]], preferred_element_type=F32)
+        y_send[j][...] = product[half:].astype(BF16).reshape(n_z, rows, SUM_WIDTHS[j])
+        sum_y(j).start()
+        own_part[j][...] = product[:half].reshape(n_z, rows, SUM_WIDTHS[j])
+
+    def pair_up(j):
+        sum_y(j).wait_recv()
+        both = own_part[j][...] + y_recv[j][...].astype(F32)
+        own_part[j][...] = both
+        z_send[j][...] = both.astype(BF16)
+        for step in range(1, n_z):
+            sum_z(j, step).start()
+
+    def finish(j):
+        total = own_part[j][z]
+        for step in range(1, n_z):
+            sum_z(j, step).wait_recv()
+            total = total + z_recv[j][step].astype(F32)
+        raw[:, spans[j]] = total
+        back_send[j][...] = fold(total[CAP:])
+        hand_back(j).start()
+
+    def collect(j):
+        hand_back(j).wait_recv()
+        out[:, spans[j]] = jnp.concatenate(
+            [raw[:CAP, spans[j]], unfold(back_recv[j][...])], axis=0
         ).astype(BF16)
 
     pair_up(0)
-    for k in range(n_c):
-        if k + 1 < n_c:
-            pair_up(k + 1)
-        finish(k)
-        if k >= 1:
-            collect(k - 1)
-    collect(n_c - 1)
+    for j in range(n_s):
+        if j + 1 < n_s:
+            pair_up(j + 1)
+        finish(j)
+        if j >= 1:
+            collect(j - 1)
+    collect(n_s - 1)
 
     for k in range(n_c):
         exchange(k).wait_send()
@@ -284,37 +304,23 @@
             along_y(k, z_from[step]).wait_send()
         for step in range(1, n_z):
             along_z(k, step).wait_send()
-            sum_z(k, step).wait_send()
-        sum_y(k).wait_send()
-        hand_back(k).wait_send()
-
-
-def combine(narrow, routes, logits, tokens, expert_out, out, coefs):
-    @pl.when(pl.program_id(0) == 0)
-    def _():
-        first, second, chosen = picks(routes[...], narrow[0])
-        values = logits[...]
-        powers = jnp.exp(values - jnp.max(values, axis=0, keepdims=True))
-        probs = powers / jnp.sum(powers, axis=0, keepdims=True)
-        weight = jnp.where(first, probs[0:1, :], 0.0) + jnp.where(second, probs[1:2, :], 0.0)
-        rest = jnp.where(chosen, weight, 0.0)
-        for piece in range(3):
-            rounded = rest.astype(BF16)
-            coefs[piece * 2 * CAP : (piece + 1) * 2 * CAP, :] = rounded
-            rest = rest - rounded.astype(F32)
-
+    for j in range(n_s):
+        for step in range(1, n_z):
+            sum_z(j, step).wait_send()
+        sum_y(j).wait_send()
+        hand_back(j).wait_send()
+
+
+def combine(coefs, tokens, expert_out, out):
     rows = expert_out[...]
-    added = lax.dot_general(
-        coefs[...],
-        jnp.concatenate([rows, rows, rows], axis=0),
-        (((0,), (0,)), ((), ())),
-        preferred_element_type=F32,
+    added = jnp.dot(
+        coefs[...], jnp.concatenate([rows, rows, rows], axis=0), preferred_element_type=F32
     )
     out[...] = (tokens[...].astype(F32) + added).astype(BF16)
 
 
 def fused(n_z, tokens, norm_gain, routes, router_logits, gate_proj, up_proj, down_proj):
-    n_c = N_CHUNKS
+    n_c, n_s = N_CHUNKS, len(SUM_WIDTHS)
     count, depth = tokens.shape
     width = depth // n_c
     units = gate_proj.shape[2]
@@ -323,66 +329,66 @@
     vmem, hbm = pl.BlockSpec(memory_space=pltpu.VMEM), pl.BlockSpec(memory_space=pl.ANY)
     dma = pltpu.SemaphoreType.DMA
     routes_t, logits_t = routes.T, router_logits.T
-    expert_out = pl.pallas_call(
-        functools.partial(experts, n_z, n_c),
-        out_shape=jax.ShapeDtypeStruct((rows, depth), BF16),
-        in_specs=[hbm, vmem, vmem, hbm, hbm, hbm],
-        out_specs=vmem,
+    expert_out, coefs = pl.pallas_call(
+        functools.partial(experts, n_z, n_c, n_s),
+        out_shape=[
+            jax.ShapeDtypeStruct((rows, depth), BF16),
+            jax.ShapeDtypeStruct((count, 3 * rows), BF16),
+        ],
+        in_specs=[hbm, vmem, vmem, vmem, hbm, hbm, hbm],
+        out_specs=[vmem, vmem],
         scratch_shapes=[
             pltpu.VMEM((n_c, count, width), BF16),
             pltpu.VMEM((n_c, units, width), BF16),
             pltpu.VMEM((n_c, units, width), BF16),
-            pltpu.VMEM((n_c, units, width), BF16),
-            pltpu.VMEM((n_c, rows, width), F32),
+            pltpu.VMEM((units, depth), BF16),
+            pltpu.VMEM((rows, depth), F32),
             pltpu.VMEM((n_c, rows, width // 2), BF16),
             pltpu.VMEM((n_c, rows, width // 2), BF16),
             pltpu.VMEM((n_c, 2 * n_z, rows, width), BF16),
             pltpu.VMEM((everyone, units), F32),
             pltpu.VMEM((everyone, units), F32),
             pltpu.VMEM((everyone, units), BF16),
-            pltpu.VMEM((n_c, n_z, rows, width), F32),
-            pltpu.VMEM((n_c, n_z, rows, width), BF16),
-            pltpu.VMEM((n_c, n_z, rows, width), BF16),
-            pltpu.VMEM((n_c, n_z, rows, width), BF16),
-            pltpu.VMEM((n_c, n_z, rows, width), BF16),
-            pltpu.VMEM((n_c, rows, width // 2), BF16),
-            pltpu.VMEM((n_c, rows, width // 2), BF16),
+            tuple(pltpu.VMEM((n_z, rows, wide), F32) for wide in SUM_WIDTHS),
+            tuple(pltpu.VMEM((n_z, rows, wide), BF16) for wide in SUM_WIDTHS),
+            tuple(pltpu.VMEM((n_z, rows, wide), BF16) for wide in SUM_WIDTHS),
+            tuple(pltpu.VMEM((n_z, rows, wide), BF16) for wide in SUM_WIDTHS),
+            tuple(pltpu.VMEM((n_z, rows, wide), BF16) for wide in SUM_WIDTHS),
+            tuple(pltpu.VMEM((rows, wide // 2), BF16) for wide in SUM_WIDTHS),
+            tuple(pltpu.VMEM((rows, wide // 2), BF16) for wide in SUM_WIDTHS),
             dma((n_c,)),
             dma((2, n_c)),
-            dma((n_c,)),
+            dma((n_s,)),
             dma((2, n_c)),
             dma((n_z, n_c)),
             dma((n_z, n_c)),
             dma((n_z, n_c)),
             dma((n_z, n_c)),
-            dma((2, n_c)),
-            dma((n_z, n_c)),
-            dma((n_z, n_c)),
-            dma((2, n_c)),
+            dma((2, n_s)),
+            dma((n_z, n_s)),
+            dma((n_z, n_s)),
+            dma((2, n_s)),
         ],
         compiler_params=pltpu.CompilerParams(
             collective_id=0, has_side_effects=True, vmem_limit_bytes=58 * 1024 * 1024
         ),
     )(
-        tokens, norm_gain.reshape(1, depth), routes_t,
+        tokens, norm_gain.reshape(1, depth), routes_t, logits_t,
         jnp.swapaxes(gate_proj, 1, 2), jnp.swapaxes(up_proj, 1, 2), down_proj,
     )
-    tile = depth // 7
-    narrow = lax.axis_index("narrow").astype(jnp.int32).reshape(1)
+    steps = 2
+    tile = depth // steps
     return pl.pallas_call(
         combine,
-        grid=(7,),
+        grid=(steps,),
         out_shape=jax.ShapeDtypeStruct(tokens.shape, BF16),
         in_specs=[
-            pl.BlockSpec(memory_space=pltpu.SMEM),
-            vmem,
             vmem,
             pl.BlockSpec((count, tile), lambda i: (0, i)),
             pl.BlockSpec((rows, tile), lambda i: (0, i)),
         ],
         out_specs=pl.BlockSpec((count, tile), lambda i: (0, i)),
-        scratch_shapes=[pltpu.VMEM((3 * rows, count), BF16)],
-    )(narrow, routes_t, logits_t, tokens, expert_out)
+    )(coefs, tokens, expert_out)
 
 
 def solution(mesh):

time: 73 us -> 68.6 us (0.940)
  Pallas kernels: 72.7 us -> 68.4 us
    pallas_call x2, Pallas kernels: 72.7 us -> 68.4 us  [the longest x1 64.8 us: fused(): pl.pallas_call(functools.partial(experts, n_z, n_c, n_s), out_shape=[jax....]
where the time goes in v2:
time: 68.6 us; the launch traced here: 68.4 us
  Pallas kernels  68.4 us (100%)
    pallas_call x1, Pallas kernels, fused(): pl.pallas_call(functools.partial(experts, n_z, n_c, n_s), out_shape=[jax....  64.8 us
    pallas_call x1, Pallas kernels, fused(): pl.pallas_call(combine, grid=(steps,), out_shape=jax.ShapeDtypeStruct(tok...  3.59 us

profile of v2, /device:TPU:0, one launch (start us, length us, event | category | flops | bytes accessed | tf_op | source)
XLA Modules:
  0.0 68.4 jit_solution(4684868194512294721)
XLA Ops:
  0.0 64.8 %shard_map.73 = (bf16[16,7168]{1,0:T(8,128)(2,1)}, bf16[208,48]{1,0:T(8,128)(2,1)}) custom-call(bf16[208,7168]{1,0:T(8,128)(2,1)} %tokens.1, f32[1,7168]{1,0:T(1,128)} %bitcast.7, s32[2,208]{1,0:T(2,128)} %bitcast.8, f32[2,208]{1,0:T(2,128)} %bitcast.9, bf16[1,608,7168]{2,1,0:T(8,128)(2,1)} %bitcast.5, bf16[1,608,7168]{2,1,0:T(8,128)(2,1)} %bitcast.6, ...), custom_call_target="tpu_custom_call" | custom-call | tf_op jit(solution)/shard_map/pallas_call | solution.py:332
  64.8 3.6 %shard_map.74 = bf16[208,7168]{1,0:T(8,128)(2,1)} custom-call(bf16[208,48]{1,0:T(8,128)(2,1)} %get-tuple-element.7.coefs, bf16[208,7168]{1,0:T(8,128)(2,1)} %tokens.1, bf16[16,7168]{1,0:T(8,128)(2,1)} %get-tuple-element.8.expert_out), custom_call_target="tpu_custom_call" | custom-call | tf_op jit(solution)/shard_map/pallas_call | solution.py:381

commit v3 on v2

--- a/solution.py
+++ b/solution.py
@@ -259,7 +259,7 @@
     hidden[...] = (gated / (1.0 + jnp.exp(-gated)) * up_acc[...]).astype(BF16)
 
     half = n_z * rows
-    for j in range(n_s):
+    def part(j):
         down_copy(j).wait()
         product = jnp.dot(hidden[...], down[:, spans[j]], preferred_element_type=F32)
         y_send[j][...] = product[half:].astype(BF16).reshape(n_z, rows, SUM_WIDTHS[j])
@@ -289,13 +289,18 @@
             [raw[:CAP, spans[j]], unfold(back_recv[j][...])], axis=0
         ).astype(BF16)
 
-    pair_up(0)
+    part(0)
+    part(1)
     for j in range(n_s):
-        if j + 1 < n_s:
-            pair_up(j + 1)
-        finish(j)
+        pair_up(j)
+        if j + 2 < n_s:
+            part(j + 2)
         if j >= 1:
-            collect(j - 1)
+            finish(j - 1)
+        if j >= 2:
+            collect(j - 2)
+    finish(n_s - 1)
+    collect(n_s - 2)
     collect(n_s - 1)
 
     for k in range(n_c):

time: 68.6 us -> 68.6 us (level)
  no operation moved by 1% of the time
where the time goes in v3:
time: 68.6 us; the launch traced here: 68.4 us
  Pallas kernels  68.4 us (100%)
    pallas_call x1, Pallas kernels, fused(): pl.pallas_call(functools.partial(experts, n_z, n_c, n_s), out_shape=[jax....  64.8 us
    pallas_call x1, Pallas kernels, fused(): pl.pallas_call(combine, grid=(steps,), out_shape=jax.ShapeDtypeStruct(tok...  3.59 us

profile of v3, /device:TPU:0, one launch (start us, length us, event | category | flops | bytes accessed | tf_op | source)
XLA Modules:
  0.0 68.4 jit_solution(15777075453819883770)
XLA Ops:
  0.0 64.8 %shard_map.73 = (bf16[16,7168]{1,0:T(8,128)(2,1)}, bf16[208,48]{1,0:T(8,128)(2,1)}) custom-call(bf16[208,7168]{1,0:T(8,128)(2,1)} %tokens.1, f32[1,7168]{1,0:T(1,128)} %bitcast.7, s32[2,208]{1,0:T(2,128)} %bitcast.8, f32[2,208]{1,0:T(2,128)} %bitcast.9, bf16[1,608,7168]{2,1,0:T(8,128)(2,1)} %bitcast.5, bf16[1,608,7168]{2,1,0:T(8,128)(2,1)} %bitcast.6, ...), custom_call_target="tpu_custom_call" | custom-call | tf_op jit(solution)/shard_map/pallas_call | solution.py:337
  64.8 3.6 %shard_map.74 = bf16[208,7168]{1,0:T(8,128)(2,1)} custom-call(bf16[208,48]{1,0:T(8,128)(2,1)} %get-tuple-element.7.coefs, bf16[208,7168]{1,0:T(8,128)(2,1)} %tokens.1, bf16[16,7168]{1,0:T(8,128)(2,1)} %get-tuple-element.8.expert_out), custom_call_target="tpu_custom_call" | custom-call | tf_op jit(solution)/shard_map/pallas_call | solution.py:386
